TPU v7x, 256 devices: a whole 4x4x8 slice. The times are simulated.
256 devices in a mesh: dp: 8 (over y, core), label: 32 (over x, z).
Axes of the slice: x: 4, y: 4, z: 8, core: 2. Of those that a mesh axis runs over, the one named last changes fastest.
Arguments:
- encoded: bfloat16 [32768, 1024], P(('dp', 'label')), may hold values from -6 to 6
- positive_clusters: int32 [32768, 4], P(('dp', 'label')), may hold values from 0 to 16383
- cluster_weight: bfloat16 [16384, 1024], P('label'), may hold values from -0.1875 to 0.1875
- shortlist: int32 [32768, 4], P(('dp', 'label')), may hold values from 0 to 511, all different within a row; in each aligned block of 128 rows (0 to 127, 128 to 255, ...) at most 2 rows name the same one
- positive_offsets: int32 [32768, 4], P(('dp', 'label')), may hold values from 0 to 127
- block_weight: bfloat16 [512, 128, 1024], P('label'), may hold values from -0.1875 to 0.1875
Outputs:
- grad_hidden: bfloat16 [32768, 1024], P(('dp', 'label'))
- grad_cluster: float32 [16384, 1024], P('label', 'dp')
- grad_block: float32 [512, 128, 1024], P('label', None, 'dp')
Inputs may be any that keep to these rules, and one draw needn't show every extreme that they name: `shortlist`: each row names 4 different blocks. Among the rows of one device no block is named more than 2 times, and in every draw some block is named exactly 2 times by the rows of some device.
All inputs are finite; a program needn't handle non-finite values.
Results may differ from a plain program's by a relative error of at most 0.018.
Values may be sent and summed in bfloat16 or wider, within the bound.
A program may use at most 128 MiB of HBM per device.

v0:
```python
import math
import jax
import jax.numpy as jnp
from jax import lax
from jax.sharding import PartitionSpec as P


def per_device(
    encoded, positive_clusters, cluster_weight, shortlist, positive_offsets, block_weight
):
    doc_rows, width = encoded.shape
    label_count = lax.axis_size("label")
    label_index = lax.axis_index("label")
    clusters_dev = cluster_weight.shape[0]
    rows_all = doc_rows * label_count
    scale = 1.0 / math.sqrt(rows_all * lax.axis_size("dp"))
    cluster_ids = label_index * clusters_dev + jnp.arange(clusters_dev, dtype=jnp.int32)
    rows = lax.all_gather(encoded, "label", axis=0, tiled=True)
    positives = lax.all_gather(positive_clusters, "label", axis=0, tiled=True)
    scores = lax.dot_general(
        rows, cluster_weight, (((1,), (1,)), ((), ())), preferred_element_type=jnp.float32
    )
    hits = jnp.any(positives[:, :, None] == cluster_ids[None, None, :], axis=1)
    delta = (jax.nn.sigmoid(scores) - hits.astype(jnp.float32)).astype(jnp.bfloat16)
    grad_sum = lax.dot_general(
        delta, rows, (((0,), (0,)), ((), ())), preferred_element_type=jnp.float32
    )
    deltas = delta
    grad_cluster, deltas = (grad_sum, deltas)
    products = jnp.dot(deltas, cluster_weight, preferred_element_type=jnp.float32)
    hidden_one = lax.psum_scatter(
        products.astype(jnp.bfloat16), "label", scatter_dimension=0, tiled=True
    ).astype(jnp.float32)
    listed = shortlist.shape[1]
    pairs = doc_rows * listed
    blocks_dev, block_len, _ = block_weight.shape
    blocks_total = blocks_dev * label_count
    capacity = max(2, 2 * pairs // blocks_total)
    slots_total = blocks_total * capacity
    flat_block = shortlist.reshape(-1)
    onehot = (flat_block[:, None] == jnp.arange(blocks_total, dtype=jnp.int32)[None, :]).astype(
        jnp.bfloat16
    )
    lower = (jnp.arange(pairs)[:, None] > jnp.arange(pairs)[None, :]).astype(jnp.bfloat16)
    earlier = jnp.dot(lower, onehot, preferred_element_type=jnp.float32)
    rank = jnp.sum(earlier * onehot.astype(jnp.float32), axis=1).astype(jnp.int32)
    slot = flat_block * capacity + rank
    source = (
        jnp.full((slots_total,), -1, jnp.int32).at[slot].set(jnp.arange(pairs, dtype=jnp.int32))
    )
    filled = source >= 0
    picked = jnp.maximum(source, 0)
    send_rows = jnp.where(filled[:, None], encoded[picked // listed], jnp.zeros((), jnp.bfloat16))
    send_offsets = jnp.where(filled, positive_offsets.reshape(-1)[picked], -1)
    send_rows = send_rows.reshape(label_count, blocks_dev * capacity, width)
    send_offsets = send_offsets.reshape(label_count, blocks_dev * capacity)
    got_rows, got_offsets = (
        lax.all_to_all(send_rows, "label", split_axis=0, concat_axis=0, tiled=True),
        lax.all_to_all(send_offsets, "label", split_axis=0, concat_axis=0, tiled=True),
    )
    arrived = got_rows.reshape(label_count, blocks_dev, capacity, width)
    offsets = got_offsets.reshape(label_count, blocks_dev, capacity)
    scores = jnp.einsum("sbcd,bld->sbcl", arrived, block_weight, preferred_element_type=jnp.float32)
    target = (offsets[..., None] == jnp.arange(block_len, dtype=jnp.int32)).astype(jnp.float32)
    delta = jnp.where((offsets >= 0)[..., None], jax.nn.sigmoid(scores) - target, 0.0).astype(
        jnp.bfloat16
    )
    back = jnp.einsum(
        "sbcl,bld->sbcd", delta, block_weight, preferred_element_type=jnp.float32
    ).astype(jnp.bfloat16)
    grad_block = jnp.einsum("sbcl,sbcd->bld", delta, arrived, preferred_element_type=jnp.float32)
    returned = lax.all_to_all(
        back.reshape(label_count, blocks_dev * capacity, width),
        "label",
        split_axis=0,
        concat_axis=0,
        tiled=True,
    )
    per_pair = returned.reshape(slots_total, width)[slot].astype(jnp.float32)
    hidden_two = jnp.sum(per_pair.reshape(doc_rows, listed, width), axis=1)
    grad_hidden = (hidden_one + hidden_two).astype(jnp.bfloat16)
    cluster_share, block_share = (
        lax.psum_scatter(
            (grad_cluster * scale).astype(jnp.bfloat16), "dp", scatter_dimension=1, tiled=True
        ).astype(jnp.float32),
        lax.psum_scatter(
            (grad_block * scale).reshape(blocks_dev * block_len, width).astype(jnp.bfloat16),
            "dp",
            scatter_dimension=1,
            tiled=True,
        ).astype(jnp.float32),
    )
    return (grad_hidden, cluster_share, block_share.reshape(blocks_dev, block_len, -1))


def solution(mesh):
    placed = (
        P(("dp", "label"), None),
        P(("dp", "label"), None),
        P("label", None),
        P(("dp", "label"), None),
        P(("dp", "label"), None),
        P("label", None, None),
    )
    return jax.shard_map(
        per_device,
        mesh=mesh,
        in_specs=placed,
        out_specs=(P(("dp", "label"), None), P("label", "dp"), P("label", None, "dp")),
        check_vma=False,
    )
```

profile of v0, /device:TPU:8, one launch (start us, length us, event | category | flops | bytes accessed | tf_op | source)
XLA Modules:
  0.0 472.1 jit_solution(16597565565228183674)
XLA Ops:
  8.0 0.0 copy-start
  8.0 0.0 copy-start.1
  8.0 0.0 all-gather.2.cloned.1.call-start
  8.1 0.7 all-gather.2.cloned.1.call-update
  8.8 0.8 copy.38
  9.5 0.7 broadcast_multiply_fusion
  10.2 0.1 copy.37
  10.3 0.1 mul.37
  10.5 0.8 copy.39
  11.2 0.1 reshape.92
  11.4 0.1 eq.42
  11.5 0.5 fusion.8
  12.0 2.4 scatter_custom_fusion
  14.5 6.9 %gather_fusion = s32[1024]{0:T(1024)S(1)} fusion(s32[512]{0:T(512)S(1)} %reshape.92, s32[1024]{0:T(1024)S(1)} %maximum_clamp_fusion), kind=kCustom, calls=%fused_computation | custom fusion | bytes 12288 | tf_op jit(solution)/shard_map/gather | solution.py:54
  21.4 0.7 all_to_all.12
  22.1 11.3 %all-to-all-start = ((s32[32,1,32]{2,1,0:T(1,128)}), s32[32,1,32]{2,1,0:T(1,128)S(1)}, u32[]{:S(2)}, u32[]{:S(2)}) async-start(s32[32,1,32]{2,1,0:T(1,128)} %bitcast.2), calls=%async_computation.1 | async-start | bytes 32768 | tf_op jit(solution)/shard_map/all_to_all | solution.py:59
  33.4 0.1 broadcast_in_dim.50
  33.5 0.0 copy-done.1
  33.5 4.1 gather_fusion.1
  37.5 1.6 broadcast_select_fusion
  39.1 4.1 all-to-all-done
  43.2 5.7 %all-to-all-start.1 = ((bf16[32,32,1024]{2,1,0:T(8,128)(2,1)}), bf16[32,32,1024]{2,1,0:T(8,128)(2,1)S(1)}, u32[]{:S(2)}, u32[]{:S(2)}) async-start(bf16[32,32,1024]{2,1,0:T(8,128)(2,1)} %broadcast_select_fusion), calls=%async_computation.2 | async-start | bytes 4194304 | tf_op jit(solution)/shard_map/all_to_all | solution.py:58
  48.9 0.0 reduce-scatter.12.cloned.1.call-start
  49.0 0.1 copy.41
  49.1 64.0 %all-to-all-done.1 = bf16[32,32,1024]{2,1,0:T(8,128)(2,1)S(1)} async-done(((bf16[32,32,1024]{2,1,0:T(8,128)(2,1)}), bf16[32,32,1024]{2,1,0:T(8,128)(2,1)S(1)}, u32[]{:S(2)}, u32[]{:S(2)}) %all-to-all-start.1) | async-done | bytes 2097184 | tf_op jit(solution)/shard_map/all_to_all | solution.py:58
  113.0 0.0 copy-start.2
  113.0 1.2 copy.42
  114.2 1.2 copy-done.2
  115.4 1.7 fusion.30
  117.1 3.2 fusion
  120.4 6.5 %copy.48 = bf16[2048,1024]{0,1:T(8,128)(2,1)} copy(bf16[2048,1024]{1,0:T(8,128)(2,1)} %bitcast.68) | data formatting | bytes 8388608
  126.8 0.0 copy-start.3
  126.8 0.0 reduce-scatter.12.cloned.1.call-update
  126.9 0.0 reduce-scatter.10.cloned.1.call-start
  126.9 0.6 copy-done.3
  127.5 48.2 %all_gather.7 = s32[4096,4]{0,1:T(4,128)S(1)} all-gather(s32[128,4]{0,1:T(4,128)S(1)} %copy-done.3), channel_id=1, replica_groups=mesh['dp'=8,'label'=32] {'label'}, dimensions={0}, use_global_device_ids=true | all-gather | bytes 67584 | tf_op jit(solution)/shard_map/all_gather | solution.py:19
  175.7 5.1 %compare_reduce_fusion = pred[4096,512]{1,0:T(8,128)(4,1)S(1)} fusion(s32[512]{0:T(512)S(1)} %iota_add_fusion, s32[4096,4]{0,1:T(4,128)S(1)} %all_gather.7), kind=kLoop, calls=%fused_computation.4 | loop fusion | flops 14680064 | bytes 2164736 | tf_op jit(solution)/shard_map/reduce_or | solution.py:23
  180.8 0.0 all-gather.2.cloned.1.call-done
  180.9 0.0 copy-done
  180.9 0.0 copy-start.4
  180.9 9.2 %subtract_convert_fusion = bf16[4096,512]{1,0:T(8,128)(2,1)S(1)} fusion(pred[4096,512]{1,0:T(8,128)(4,1)S(1)} %compare_reduce_fusion, bf16[4096,1024]{1,0:T(8,128)(2,1)} %all-gather.2.cloned.1.call-done, bf16[512,1024]{1,0:T(8,128)(2,1)S(1)} %copy-done), kind=kOutput, calls=%fused_computation.7 | convolution fusion | flops 4307550208 | bytes 15728640 | tf_op jit(solution)/shard_map/dot_general | solution.py:20
  190.1 0.0 copy-start.5
  190.1 1.9 copy-done.5
  192.0 0.0 copy-done.4
  192.0 4.5 multiply_convert_fusion
  196.5 1.3 copy.46
  197.9 0.0 reduce-scatter.10.cloned.1.call-update
  197.9 0.3 reduce-scatter.8.cloned.1.call-start
  198.1 9.0 %convolution_convert_fusion = bf16[4096,1024]{1,0:T(8,128)(2,1)} fusion(bf16[4096,512]{1,0:T(8,128)(2,1)} %copy-done.5, bf16[512,1024]{1,0:T(8,128)(2,1)S(1)} %copy-done), kind=kOutput, calls=%fused_computation.8 | convolution fusion | flops 4299161600 | bytes 13631488 | tf_op jit(solution)/shard_map/dot_general | solution.py:30
  207.1 0.0 reduce-scatter.8.cloned.1.call-update
  207.2 2.9 fusion.5
  210.1 2.5 copy.43
  212.6 5.5 %all-to-all-start.2 = ((bf16[32,32,1024]{2,1,0:T(8,128)(2,1)}), bf16[32,32,1024]{2,1,0:T(8,128)(2,1)S(1)}, u32[]{:S(2)}, u32[]{:S(2)}) async-start(bf16[32,32,1024]{2,1,0:T(8,128)(2,1)} %copy.43), calls=%async_computation.3 | async-start | bytes 4194304 | tf_op jit(solution)/shard_map/all_to_all | solution.py:72
  218.2 39.4 %all-to-all-done.2 = bf16[32,32,1024]{2,1,0:T(8,128)(2,1)S(1)} async-done(((bf16[32,32,1024]{2,1,0:T(8,128)(2,1)}), bf16[32,32,1024]{2,1,0:T(8,128)(2,1)S(1)}, u32[]{:S(2)}, u32[]{:S(2)}) %all-to-all-start.2) | async-done | bytes 2097184 | tf_op jit(solution)/shard_map/all_to_all | solution.py:72
  257.5 2.8 gather_fusion.2
  260.3 1.7 reshape.99
  262.0 2.2 reduce_sum.19
  264.3 0.0 reduce-scatter.12.cloned.1.call-done
  264.3 1.3 copy.49
  265.6 1.1 convert.2
  266.7 1.0 copy.47
  267.7 0.7 convert_element_type.83
  268.4 194.2 %reduce-scatter.8.cloned.1.call-done = bf16[128,1024]{1,0:T(8,128)(2,1)} async-done(((bf16[4096,1024]{1,0:T(8,128)(2,1)}), bf16[128,1024]{1,0:T(8,128)(2,1)}) %reduce-scatter.8.cloned.1.call-update) | async-done | bytes 262160 | tf_op jit(solution)/shard_map/reduce_scatter | solution.py:31
  462.7 1.9 add_convert_fusion
  (9 shorter events, 0.1 us)
Async XLA Ops:
  8.0 172.9 %copy-start = (bf16[512,1024]{1,0:T(8,128)(2,1)S(1)}, bf16[512,1024]{1,0:T(8,128)(2,1)}, u32[]{:S(2)}) copy-start(bf16[512,1024]{1,0:T(8,128)(2,1)} %param.8) | copy-start | bytes 3145732
  8.0 25.5 %copy-start.1 = (bf16[128,1024]{1,0:T(8,128)(2,1)S(1)}, bf16[128,1024]{1,0:T(8,128)(2,1)}, u32[]{:S(2)}) copy-start(bf16[128,1024]{1,0:T(8,128)(2,1)} %param.6) | copy-start | bytes 786436
  8.0 172.8 %all-gather.2.cloned.1.call-start = ((), (), s32[]{:S(2)}) async-start(), calls=%async_computation.6 | async-start | bytes 8650752 | tf_op jit(solution)/shard_map/all_gather | solution.py:18
  22.1 21.1 %all-to-all-start = ((s32[32,1,32]{2,1,0:T(1,128)}), s32[32,1,32]{2,1,0:T(1,128)S(1)}, u32[]{:S(2)}, u32[]{:S(2)}) async-start(s32[32,1,32]{2,1,0:T(1,128)} %bitcast.2), calls=%async_computation.1 | async-start | bytes 32768 | tf_op jit(solution)/shard_map/all_to_all | solution.py:59
  43.2 69.8 %all-to-all-start.1 = ((bf16[32,32,1024]{2,1,0:T(8,128)(2,1)}), bf16[32,32,1024]{2,1,0:T(8,128)(2,1)S(1)}, u32[]{:S(2)}, u32[]{:S(2)}) async-start(bf16[32,32,1024]{2,1,0:T(8,128)(2,1)} %broadcast_select_fusion), calls=%async_computation.2 | async-start | bytes 4194304 | tf_op jit(solution)/shard_map/all_to_all | solution.py:58
  48.9 215.3 %reduce-scatter.12.cloned.1.call-start = ((), (), s32[]{:S(2)}) async-start(), calls=%async_computation.9 | async-start | bytes 4718592
  113.0 2.3 copy-start.2
  126.8 0.7 copy-start.3
  126.9 139.8 %reduce-scatter.10.cloned.1.call-start = ((), (), s32[]{:S(2)}) async-start(), calls=%async_computation.8 | async-start | bytes 1179648
  180.9 11.1 %copy-start.4 = (bf16[4096,1024]{1,0:T(8,128)(2,1)S(1)}, bf16[4096,1024]{1,0:T(8,128)(2,1)}, u32[]{:S(2)}) copy-start(bf16[4096,1024]{1,0:T(8,128)(2,1)} %all-gather.2.cloned.1.call-done) | copy-start | bytes 25165828
  190.1 1.9 copy-start.5
  197.9 264.8 %reduce-scatter.8.cloned.1.call-start = ((), (), s32[]{:S(2)}) async-start(), calls=%async_computation.7 | async-start | bytes 8650752 | tf_op jit(solution)/shard_map/reduce_scatter | solution.py:31
  212.6 44.9 %all-to-all-start.2 = ((bf16[32,32,1024]{2,1,0:T(8,128)(2,1)}), bf16[32,32,1024]{2,1,0:T(8,128)(2,1)S(1)}, u32[]{:S(2)}, u32[]{:S(2)}) async-start(bf16[32,32,1024]{2,1,0:T(8,128)(2,1)} %copy.43), calls=%async_computation.3 | async-start | bytes 4194304 | tf_op jit(solution)/shard_map/all_to_all | solution.py:72
Sparse Core Ops, SparseCore 0:
  11.4 126.3 all-gather.1
Sparse Core Ops, SparseCore 1:
  126.9 34.5 reduce-scatter.11
  198.0 28.3 reduce-scatter.9
  230.2 232.4 reduce-scatter.7
where the time goes:
time: 473 us; the launch traced here: 472 us
  waiting for transfers between devices  302 us (64%)
  blocking collectives  48.2 us (10%)
  local copies, waits for them, and re-layouts  38.2 us (8%)
  matrix products  31.1 us (7%)
  starting transfers between devices  23 us (5%)
  between operations  15.9 us (3%)
  other arithmetic  13.4 us (3%)
    reduce_scatter x1, waiting for transfers between devices, per_device(): lax.psum_scatter(products.astype(jnp.bfloat16), 'label', scatter_dimensio...  194 us
    all_to_all x1, waiting for transfers between devices, per_device(): lax.all_to_all(send_rows, 'label', split_axis=0, concat_axis=0, tiled=True)  64 us
    all_gather x1, blocking collectives, per_device(): positives = lax.all_gather(positive_clusters, 'label', axis=0, tiled=True)  48.2 us
    all_to_all x1, waiting for transfers between devices, per_device(): lax.all_to_all(back.reshape(label_count, blocks_dev * capacity, width), '...  39.4 us
    unnamed x18, local copies, waits for them, and re-layouts  15.4 us
    all_to_all x1, starting transfers between devices, per_device(): lax.all_to_all(send_offsets, 'label', split_axis=0, concat_axis=0, tiled=...  11.3 us
  transfers between devices with their start and end apart: 7, of which 4 were waited for; matrix products, arithmetic and copies ran while one was open for 16% of the time, Pallas kernels for 0%

commit v1 on v0

--- a/solution.py
+++ b/solution.py
@@ -3,6 +3,25 @@
 import jax.numpy as jnp
 from jax import lax
 from jax.sharding import PartitionSpec as P
+
+
+def divide_cycles(view, which_dim):
+    u_next = list(view.shape[1:])
+    u_next[which_dim] *= view.shape[0]
+    return jnp.moveaxis(view, 0, which_dim).reshape(u_next)
+
+
+def define_ticks_over_axis(own_rows, link_axis):
+    degree = jax.lax.axis_size(link_axis)
+    block_next = own_rows[None]
+    for tick in range(degree.bit_length() - 1):
+        val2 = 1 << tick
+        w2 = jax.lax.ppermute(block_next, link_axis, [(nth, nth ^ val2) for nth in range(degree)])
+        r_now = jnp.stack([block_next, w2], 0)
+        a_next = jax.lax.axis_index(link_axis)
+        long_array = a_next >> tick & 1
+        block_next = jnp.where(long_array == 0, r_now, r_now[::-1]).reshape(-1, *own_rows.shape)
+    return block_next
 
 
 def per_device(
@@ -16,7 +35,7 @@
     scale = 1.0 / math.sqrt(rows_all * lax.axis_size("dp"))
     cluster_ids = label_index * clusters_dev + jnp.arange(clusters_dev, dtype=jnp.int32)
     rows = lax.all_gather(encoded, "label", axis=0, tiled=True)
-    positives = lax.all_gather(positive_clusters, "label", axis=0, tiled=True)
+    positives = divide_cycles(define_ticks_over_axis(positive_clusters, "label"), 0)
     scores = lax.dot_general(
         rows, cluster_weight, (((1,), (1,)), ((), ())), preferred_element_type=jnp.float32
     )

time: 473 us -> 454 us (0.960)
  blocking collectives: 48.2 us -> 0 us
  waiting for transfers between devices: 302 us -> 320 us
  starting transfers between devices: 23 us -> 35 us
    all_gather x1 -> x0, blocking collectives: 48.2 us -> none  [per_device(): positives = lax.all_gather(positive_clusters, 'label', axis=0, tiled=True)]
    ppermute x0 -> x5, waiting for transfers between devices: none -> 13.9 us  [define_ticks_over_axis(): jax.lax.ppermute(block_next, link_axis, [(nth, nth ^ val2) for nth in ran...]
    ppermute x0 -> x5, starting transfers between devices: none -> 11.4 us  [define_ticks_over_axis(): jax.lax.ppermute(block_next, link_axis, [(nth, nth ^ val2) for nth in ran...]
    all_to_all x1, waiting for transfers between devices: 39.4 us -> 50 us  [per_device(): lax.all_to_all(back.reshape(label_count, blocks_dev * capacity, width), '...]
    reduce_scatter x1, waiting for transfers between devices: 194 us -> 187 us  [per_device(): lax.psum_scatter(products.astype(jnp.bfloat16), 'label', scatter_dimensio...]
    unnamed x18 -> x19, local copies, waits for them, and re-layouts: 15.4 us -> 15.5 us
  transfers between devices with their start and end apart: 7 -> 12, of which waited for: 4 -> 9; matrix products, arithmetic and copies ran while one was open for 16% -> 17% of each run, Pallas kernels for 0% -> 0%
where the time goes in v1:
time: 454 us; the launch traced here: 453 us
  waiting for transfers between devices  320 us (70%)
  local copies, waits for them, and re-layouts  38.3 us (8%)
  starting transfers between devices  35 us (8%)
  matrix products  31.2 us (7%)
  between operations  15.9 us (4%)
  other arithmetic  13.4 us (3%)
    reduce_scatter x1, waiting for transfers between devices, per_device(): lax.psum_scatter(products.astype(jnp.bfloat16), 'label', scatter_dimensio...  187 us
    all_to_all x1, waiting for transfers between devices, per_device(): lax.all_to_all(send_rows, 'label', split_axis=0, concat_axis=0, tiled=True)  64 us
    all_to_all x1, waiting for transfers between devices, per_device(): lax.all_to_all(back.reshape(label_count, blocks_dev * capacity, width), '...  50 us
    unnamed x19, local copies, waits for them, and re-layouts  15.5 us
    ppermute x5, waiting for transfers between devices, define_ticks_over_axis(): jax.lax.ppermute(block_next, link_axis, [(nth, nth ^ val2) for nth in ran...  13.9 us
    ppermute x5, starting transfers between devices, define_ticks_over_axis(): jax.lax.ppermute(block_next, link_axis, [(nth, nth ^ val2) for nth in ran...  11.4 us
    all_to_all x1, starting transfers between devices, per_device(): lax.all_to_all(send_offsets, 'label', split_axis=0, concat_axis=0, tiled=...  11.3 us
    dot_general x1, matrix products, per_device(): lax.dot_general(rows, cluster_weight, (((1,), (1,)), ((), ())), preferred...  9.33 us
  transfers between devices with their start and end apart: 12, of which 9 were waited for; matrix products, arithmetic and copies ran while one was open for 17% of the time, Pallas kernels for 0%

profile of v1, /device:TPU:8, one launch (start us, length us, event | category | flops | bytes accessed | tf_op | source)
XLA Modules:
  0.0 453.5 jit_solution(13284545659838967802)
XLA Ops:
  8.0 0.0 copy-start
  8.0 0.0 all-gather.2.cloned.1.call-start
  8.1 0.7 all-gather.2.cloned.1.call-update
  8.8 0.8 copy.45
  9.5 0.7 broadcast_multiply_fusion
  10.2 0.1 copy.44
  10.3 0.1 mul.37
  10.5 0.8 copy.46
  11.2 0.1 reshape.108
  11.4 0.1 eq.65
  11.5 0.5 fusion.8
  12.0 2.4 scatter_custom_fusion
  14.5 6.9 %gather_fusion = s32[1024]{0:T(1024)S(1)} fusion(s32[512]{0:T(512)S(1)} %reshape.108, s32[1024]{0:T(1024)S(1)} %maximum_clamp_fusion), kind=kCustom, calls=%fused_computation | custom fusion | bytes 12288 | tf_op jit(solution)/shard_map/gather | solution.py:73
  21.4 0.7 all_to_all.12
  22.1 11.3 %all-to-all-start = ((s32[32,1,32]{2,1,0:T(1,128)}), s32[32,1,32]{2,1,0:T(1,128)S(1)}, u32[]{:S(2)}, u32[]{:S(2)}) async-start(s32[32,1,32]{2,1,0:T(1,128)} %bitcast.17), calls=%async_computation.1 | async-start | bytes 32768 | tf_op jit(solution)/shard_map/all_to_all | solution.py:78
  33.4 0.1 broadcast_in_dim.53
  33.5 4.1 gather_fusion.1
  37.5 1.6 broadcast_select_fusion
  39.1 4.1 all-to-all-done
  43.2 5.7 %all-to-all-start.1 = ((bf16[32,32,1024]{2,1,0:T(8,128)(2,1)}), bf16[32,32,1024]{2,1,0:T(8,128)(2,1)S(1)}, u32[]{:S(2)}, u32[]{:S(2)}) async-start(bf16[32,32,1024]{2,1,0:T(8,128)(2,1)} %broadcast_select_fusion), calls=%async_computation.2 | async-start | bytes 4194304 | tf_op jit(solution)/shard_map/all_to_all | solution.py:77
  48.9 0.0 reduce-scatter.12.cloned.1.call-start
  49.0 0.1 copy.48
  49.1 64.0 %all-to-all-done.1 = bf16[32,32,1024]{2,1,0:T(8,128)(2,1)S(1)} async-done(((bf16[32,32,1024]{2,1,0:T(8,128)(2,1)}), bf16[32,32,1024]{2,1,0:T(8,128)(2,1)S(1)}, u32[]{:S(2)}, u32[]{:S(2)}) %all-to-all-start.1) | async-done | bytes 2097184 | tf_op jit(solution)/shard_map/all_to_all | solution.py:77
  113.1 1.2 copy.49
  114.2 1.2 copy-done.2
  115.4 1.7 fusion.30
  117.1 3.2 fusion
  120.3 6.5 %copy.55 = bf16[2048,1024]{0,1:T(8,128)(2,1)} copy(bf16[2048,1024]{1,0:T(8,128)(2,1)} %bitcast.94) | data formatting | bytes 8388608
  126.9 0.0 reduce-scatter.12.cloned.1.call-update
  126.9 0.0 reduce-scatter.10.cloned.1.call-start
  126.9 0.6 copy-done.3
  127.5 1.6 collective-permute-start
  129.2 2.0 collective-permute-done
  131.2 2.4 collective-permute-start.1
  133.6 2.2 collective-permute-done.1
  135.8 3.3 collective-permute-start.2
  139.1 4.3 collective-permute-done.2
  143.4 1.1 collective-permute-start.3
  144.5 2.7 collective-permute-done.3
  147.3 2.9 collective-permute-start.4
  150.2 2.8 collective-permute-done.4
  153.0 5.1 %compare_reduce_fusion = pred[4096,512]{1,0:T(8,128)(4,1)S(1)} fusion(s32[512]{0:T(512)S(1)} %iota_add_fusion, s32[4096,4]{0,1:T(4,128)S(1)} %bitcast.102), kind=kLoop, calls=%fused_computation.4 | loop fusion | flops 14680064 | bytes 2164736 | tf_op jit(solution)/shard_map/reduce_or | solution.py:42
  158.2 0.0 all-gather.2.cloned.1.call-done
  158.2 9.3 %subtract_convert_fusion = bf16[4096,512]{1,0:T(8,128)(2,1)S(1)} fusion(pred[4096,512]{1,0:T(8,128)(4,1)S(1)} %compare_reduce_fusion, bf16[4096,1024]{1,0:T(8,128)(2,1)} %all-gather.2.cloned.1.call-done, bf16[512,1024]{1,0:T(8,128)(2,1)S(1)} %copy-done), kind=kOutput, calls=%fused_computation.7 | convolution fusion | flops 4307550208 | bytes 15728640 | tf_op jit(solution)/shard_map/dot_general | solution.py:39
  167.6 1.9 copy-done.5
  169.5 4.5 multiply_convert_fusion
  174.0 1.3 copy.53
  175.3 0.0 reduce-scatter.10.cloned.1.call-update
  175.4 0.3 reduce-scatter.8.cloned.1.call-start
  175.6 9.0 %convolution_convert_fusion = bf16[4096,1024]{1,0:T(8,128)(2,1)} fusion(bf16[4096,512]{1,0:T(8,128)(2,1)} %copy-done.5, bf16[512,1024]{1,0:T(8,128)(2,1)S(1)} %copy-done), kind=kOutput, calls=%fused_computation.8 | convolution fusion | flops 4299161600 | bytes 13631488 | tf_op jit(solution)/shard_map/dot_general | solution.py:49
  184.6 0.0 reduce-scatter.8.cloned.1.call-update
  184.6 2.9 fusion.5
  187.6 2.5 copy.50
  190.0 6.1 %all-to-all-start.2 = ((bf16[32,32,1024]{2,1,0:T(8,128)(2,1)}), bf16[32,32,1024]{2,1,0:T(8,128)(2,1)S(1)}, u32[]{:S(2)}, u32[]{:S(2)}) async-start(bf16[32,32,1024]{2,1,0:T(8,128)(2,1)} %copy.50), calls=%async_computation.3 | async-start | bytes 4194304 | tf_op jit(solution)/shard_map/all_to_all | solution.py:91
  196.2 50.0 %all-to-all-done.2 = bf16[32,32,1024]{2,1,0:T(8,128)(2,1)S(1)} async-done(((bf16[32,32,1024]{2,1,0:T(8,128)(2,1)}), bf16[32,32,1024]{2,1,0:T(8,128)(2,1)S(1)}, u32[]{:S(2)}, u32[]{:S(2)}) %all-to-all-start.2) | async-done | bytes 2097184 | tf_op jit(solution)/shard_map/all_to_all | solution.py:91
  246.2 2.8 gather_fusion.2
  249.0 1.7 reshape.115
  250.7 2.2 reduce_sum.19
  252.9 1.3 copy.56
  254.2 1.1 convert.2
  255.3 1.0 copy.54
  256.3 0.7 convert_element_type.83
  257.1 186.9 %reduce-scatter.8.cloned.1.call-done = bf16[128,1024]{1,0:T(8,128)(2,1)} async-done(((bf16[4096,1024]{1,0:T(8,128)(2,1)}), bf16[128,1024]{1,0:T(8,128)(2,1)}) %reduce-scatter.8.cloned.1.call-update) | async-done | bytes 262160 | tf_op jit(solution)/shard_map/reduce_scatter | solution.py:50
  444.0 1.9 add_convert_fusion
  (31 shorter events, 0.2 us)
Async XLA Ops:
  8.0 150.2 %copy-start = (bf16[512,1024]{1,0:T(8,128)(2,1)S(1)}, bf16[512,1024]{1,0:T(8,128)(2,1)}, u32[]{:S(2)}) copy-start(bf16[512,1024]{1,0:T(8,128)(2,1)} %param.8) | copy-start | bytes 3145732
  8.0 25.5 %copy-start.1 = (bf16[128,1024]{1,0:T(8,128)(2,1)S(1)}, bf16[128,1024]{1,0:T(8,128)(2,1)}, u32[]{:S(2)}) copy-start(bf16[128,1024]{1,0:T(8,128)(2,1)} %param.6) | copy-start | bytes 786436
  8.0 150.2 %all-gather.2.cloned.1.call-start = ((), (), s32[]{:S(2)}) async-start(), calls=%async_computation.6 | async-start | bytes 8650752 | tf_op jit(solution)/shard_map/all_gather | solution.py:37
  22.1 21.1 %all-to-all-start = ((s32[32,1,32]{2,1,0:T(1,128)}), s32[32,1,32]{2,1,0:T(1,128)S(1)}, u32[]{:S(2)}, u32[]{:S(2)}) async-start(s32[32,1,32]{2,1,0:T(1,128)} %bitcast.17), calls=%async_computation.1 | async-start | bytes 32768 | tf_op jit(solution)/shard_map/all_to_all | solution.py:78
  43.2 69.9 %all-to-all-start.1 = ((bf16[32,32,1024]{2,1,0:T(8,128)(2,1)}), bf16[32,32,1024]{2,1,0:T(8,128)(2,1)S(1)}, u32[]{:S(2)}, u32[]{:S(2)}) async-start(bf16[32,32,1024]{2,1,0:T(8,128)(2,1)} %broadcast_select_fusion), calls=%async_computation.2 | async-start | bytes 4194304 | tf_op jit(solution)/shard_map/all_to_all | solution.py:77
  48.9 204.0 %reduce-scatter.12.cloned.1.call-start = ((), (), s32[]{:S(2)}) async-start(), calls=%async_computation.9 | async-start | bytes 4718592
  113.1 2.3 copy-start.2
  126.9 0.7 copy-start.3
  126.9 128.4 %reduce-scatter.10.cloned.1.call-start = ((), (), s32[]{:S(2)}) async-start(), calls=%async_computation.8 | async-start | bytes 1179648
  127.5 3.6 collective-permute-start
  131.2 4.6 %collective-permute-start.1 = (s32[2,128,4]{1,2,0:T(4,128)S(1)}, s32[2,128,4]{1,2,0:T(4,128)S(1)}, u32[]{:S(2)}, u32[]{:S(2)}) collective-permute-start(s32[2,128,4]{1,2,0:T(4,128)S(1)} %get-tuple-element.8), channel_id=1, source_target_pairs={{0,2},{1,3},{2,0},{3,1},{4,6},{5,7},{6,4},{7,5},{8,10},{9,11},{10,... | collective-permute-start | bytes 12296 | tf_op jit(solution)/shard_map/ppermute | solution.py:19
  135.8 7.6 %collective-permute-start.2 = (s32[4,128,4]{1,2,0:T(4,128)S(1)}, s32[4,128,4]{1,2,0:T(4,128)S(1)}, u32[]{:S(2)}, u32[]{:S(2)}) collective-permute-start(s32[4,128,4]{1,2,0:T(4,128)S(1)} %bitcast.109), channel_id=1, source_target_pairs={{0,4},{1,5},{2,6},{3,7},{4,0},{5,1},{6,2},{7,3},{8,12},{9,13},{10,... | collective-permute-start | bytes 24584 | tf_op jit(solution)/shard_map/ppermute | solution.py:19
  143.4 3.8 collective-permute-start.3
  147.3 5.7 %collective-permute-start.4 = (s32[16,128,4]{1,0,2:T(8,128)S(1)}, s32[16,128,4]{1,0,2:T(8,128)S(1)}, u32[]{:S(2)}, u32[]{:S(2)}) collective-permute-start(s32[16,128,4]{1,0,2:T(8,128)S(1)} %get-tuple-element.6), channel_id=1, source_target_pairs={{0,16},{1,17},{2,18},{3,19},{4,20},{5,21},{6,22},{7,23},{8,24},{9,... | collective-permute-start | bytes 98312 | tf_op jit(solution)/shard_map/ppermute | solution.py:19
  158.2 11.3 %copy-start.4 = (bf16[4096,1024]{1,0:T(8,128)(2,1)S(1)}, bf16[4096,1024]{1,0:T(8,128)(2,1)}, u32[]{:S(2)}) copy-start(bf16[4096,1024]{1,0:T(8,128)(2,1)} %all-gather.2.cloned.1.call-done) | copy-start | bytes 25165828
  167.6 1.9 copy-start.5
  175.4 268.6 %reduce-scatter.8.cloned.1.call-start = ((), (), s32[]{:S(2)}) async-start(), calls=%async_computation.7 | async-start | bytes 8650752 | tf_op jit(solution)/shard_map/reduce_scatter | solution.py:50
  190.0 56.2 %all-to-all-start.2 = ((bf16[32,32,1024]{2,1,0:T(8,128)(2,1)}), bf16[32,32,1024]{2,1,0:T(8,128)(2,1)S(1)}, u32[]{:S(2)}, u32[]{:S(2)}) async-start(bf16[32,32,1024]{2,1,0:T(8,128)(2,1)} %copy.50), calls=%async_computation.3 | async-start | bytes 4194304 | tf_op jit(solution)/shard_map/all_to_all | solution.py:91
Sparse Core Ops, SparseCore 0:
  11.4 126.2 all-gather.1
Sparse Core Ops, SparseCore 1:
  127.0 34.5 reduce-scatter.11
  175.5 28.8 reduce-scatter.9
  208.2 235.7 reduce-scatter.7
